TPU v7x, 32 devices: a whole 2x2x4 slice. The times are simulated.
32 devices in a mesh: leaf: 32 (over z, y, x, core).
Axes of the slice: x: 2, y: 2, z: 4, core: 2. Of those that a mesh axis runs over, the one named last changes fastest.
Arguments:
- probes: float32 [32768, 1024], P('leaf'), may hold values from -6 to 6
- leaf_basis: float32 [64, 512, 64], P('leaf'), may hold values from -0.25 to 0.25
- leaf_transfer: float32 [64, 64, 64], P('leaf'), may hold values from -0.75 to 0.75
- cluster_transfer: float32 [16, 64, 64], replicated, may hold values from -0.75 to 0.75
- couple_one: float32 [128, 64, 64], P('leaf'), may hold values from -0.75 to 0.75
- pairs_one: int32 [128], P('leaf'), may hold values from 0 to 15, as said below
- count_one: int32 [16], replicated, may hold values from 0 to 8
- couple_two: float32 [32, 64, 64], P('leaf'), may hold values from -0.75 to 0.75
- pairs_two: int32 [32], P('leaf'), may hold values from 0 to 3, as said below
- count_two: int32 [4], replicated, may hold values from 0 to 2
- near_blocks: float32 [64, 3, 512, 512], P('leaf'), may hold values from -0.15625 to 0.15625
- near_list: int32 [64, 3], P('leaf'), may hold values from 0 to 63, as said below
Outputs:
- kernel_times: float32 [32768, 1024], P('leaf')
Inputs may be any that keep to these rules, and one draw needn't show every extreme that they name: `pairs_one`: for slots k < count_one[c], the partners of cluster c are distinct clusters j with |j - c| >= 2 and |j // 4 - c // 4| <= 1; the other slots hold c itself. `pairs_two`: for slots k < count_two[q], the partners of cluster q are distinct clusters j with |j - q| >= 2 and |j // 4 - q // 4| <= 1; the other slots hold q itself. near_list[i, 0] is i, and every entry of row i lies within i - 2 to i + 2.
All inputs are finite; a program needn't handle non-finite values.
Results may differ from a plain program's by a relative error of at most 0.000086.
Values sent between devices are 32-bit elements; how exact they have to be, the bound alone decides.
A program may use at most 128 MiB of HBM per device.

v0:
```python
import jax
import jax.numpy as jnp
from jax import lax
from jax.sharding import PartitionSpec as P

partner_offsets = (-7, -6, -5, -4, -3, -2, 2, 3, 4, 5, 6, 7)


def swapped(shard, axis, apart):
    return lax.ppermute(shard, axis, [(i, i ^ 1 << apart) for i in range(lax.axis_size(axis))])


def shifted(shard, axis, by):
    peers = lax.axis_size(axis)
    pairs = [(i, i + by) for i in range(peers) if 0 <= i + by < peers]
    return lax.ppermute(shard, axis, pairs)


def padded_2(shard, sides, width):
    for axis, dim in sides:
        peers, length = (lax.axis_size(axis), shard.shape[dim])
        up = [(i, (i + 1) % peers) for i in range(peers - 1)]
        down = [(j, i) for i, j in up]
        last = lax.slice_in_dim(shard, length - width, length, axis=dim)
        leading = lax.slice_in_dim(shard, 0, width, axis=dim)
        before = lax.ppermute(last, axis, up)
        after = lax.ppermute(leading, axis, down)
        shard = jnp.concatenate([before, shard, after], axis=dim)
    return shard


def upper_bit(position, bit_index):
    return position >> bit_index & 1 == 1


def halve_sum(values, position, first_bit, last_bit):
    for bit_index in range(first_bit, last_bit):
        half = values.shape[-1] // 2
        lower = values[:, :half]
        upper = values[:, half:]
        upper_side = upper_bit(position, bit_index)
        keep = jnp.where(upper_side, upper, lower)
        give = jnp.where(upper_side, lower, upper)
        values = keep + swapped(give, "leaf", bit_index)
    return values


def join_columns(values, position, bit_list):
    for bit_index in bit_list:
        other = swapped(values, "leaf", bit_index)
        upper_side = upper_bit(position, bit_index)
        values = jnp.where(
            upper_side,
            jnp.concatenate([other, values], axis=1),
            jnp.concatenate([values, other], axis=1),
        )
    return values


def gather_slots(coupling, partner_ids, position, last_bit):
    for bit_index in range(last_bit):
        other_blocks = swapped(coupling, "leaf", bit_index)
        other_ids = swapped(partner_ids, "leaf", bit_index)
        upper_side = upper_bit(position, bit_index)
        coupling = jnp.where(
            upper_side,
            jnp.concatenate([other_blocks, coupling], axis=0),
            jnp.concatenate([coupling, other_blocks], axis=0),
        )
        partner_ids = jnp.where(
            upper_side,
            jnp.concatenate([other_ids, partner_ids], axis=0),
            jnp.concatenate([partner_ids, other_ids], axis=0),
        )
    return (coupling, partner_ids)


def fetch_shares(coeffs, stride, devices):
    usable = [offset for offset in partner_offsets if abs(offset) * stride < devices]
    stacked = jnp.stack([shifted(coeffs, "leaf", -offset * stride) for offset in usable])
    return (stacked, jnp.array(usable, jnp.int32))


def make_picker(stacked, usable):
    highest = lax.Precision.HIGHEST

    def picker(partner_ids, owners):
        select = ((partner_ids - owners)[:, None] == usable[None, :]).astype(jnp.float32)
        return jnp.einsum("ko,orp->krp", select, stacked, precision=highest)

    return picker


def couple_level(coupling, partner_ids, counts, picker, first_slot, slots_each):
    highest = lax.Precision.HIGHEST
    slot_total = partner_ids.shape[0]
    slot_index = first_slot + jnp.arange(slot_total, dtype=jnp.int32)
    owners = slot_index // slots_each
    within = slot_index % slots_each
    valid = (within < jnp.take(counts, owners)).astype(jnp.float32)
    partner = picker(partner_ids, owners) * valid[:, None, None]
    return jnp.einsum("krs,ksp->rp", coupling, partner, precision=highest)


def body(
    probes,
    leaf_basis,
    leaf_transfer,
    cluster_transfer,
    couple_one,
    pairs_one,
    count_one,
    couple_two,
    pairs_two,
    count_two,
    near_blocks,
    near_list,
):
    highest = lax.Precision.HIGHEST
    devices = lax.axis_size("leaf")
    position = lax.axis_index("leaf")
    leaf_count, leaf_size, rank_size = leaf_basis.shape
    width = probes.shape[1]
    blocks = probes.reshape(leaf_count, leaf_size, width)
    leaf_coef = jnp.einsum("lnr,lnp->lrp", leaf_basis, blocks, precision=highest)
    part_one = jnp.einsum("lrs,lrp->sp", leaf_transfer, leaf_coef, precision=highest)
    stride_one = 4 // leaf_count
    stride_two = 16 // leaf_count
    bits_one = stride_one.bit_length() - 1
    bits_two = stride_two.bit_length() - 1
    own_one = position * leaf_count // 4
    own_two = position * leaf_count // 16
    own_transfer = lax.dynamic_index_in_dim(cluster_transfer, own_one, 0, keepdims=False)
    slots_one = pairs_one.shape[0]
    slots_each = slots_one * stride_one
    share_one = halve_sum(part_one, position, 0, bits_one)
    lifted = jnp.einsum("rs,rp->sp", own_transfer, share_one, precision=highest)
    share_two = halve_sum(lifted, position, bits_one, bits_two)
    stacked_one, usable_one = fetch_shares(share_one, stride_one, devices)
    stacked_two, usable_two = fetch_shares(share_two, stride_two, devices)
    blocks_one, ids_one = gather_slots(couple_one, pairs_one, position, bits_one)
    blocks_two, ids_two = gather_slots(couple_two, pairs_two, position, bits_two)
    far_one = couple_level(
        blocks_one,
        ids_one,
        count_one,
        make_picker(stacked_one, usable_one),
        own_one * slots_each,
        slots_each,
    )
    share_far = couple_level(
        blocks_two,
        ids_two,
        count_two,
        make_picker(stacked_two, usable_two),
        own_two * slots_each,
        slots_each,
    )
    far_two = join_columns(share_far, position, list(range(bits_two - 1, bits_one - 1, -1)))
    down_share = far_one + jnp.einsum("rs,sp->rp", own_transfer, far_two, precision=highest)
    down_one = join_columns(down_share, position, list(range(bits_one - 1, -1, -1)))
    child = jnp.einsum("lrs,sp->lrp", leaf_transfer, down_one, precision=highest)
    far_rows = jnp.einsum("lnr,lrp->lnp", leaf_basis, child, precision=highest)
    padded = padded_2(probes, (("leaf", 0),), leaf_count * leaf_size)
    padded = padded.reshape(3 * leaf_count, leaf_size, width)
    local_index = near_list - (position * leaf_count - leaf_count)
    near_rows = jnp.take(padded, local_index.reshape(-1), axis=0).reshape(
        leaf_count, -1, leaf_size, width
    )
    near_part = jnp.einsum("lmab,lmbp->lap", near_blocks, near_rows, precision=highest)
    return (far_rows + near_part).reshape(-1, width)


def solution(mesh):
    return jax.shard_map(
        body,
        mesh=mesh,
        in_specs=(
            P("leaf", None),
            P("leaf", None, None),
            P("leaf", None, None),
            P(),
            P("leaf", None, None),
            P("leaf"),
            P(),
            P("leaf", None, None),
            P("leaf"),
            P(),
            P("leaf", None, None, None),
            P("leaf", None),
        ),
        out_specs=P("leaf", None),
        check_vma=False,
    )
```

profile of v0, /device:TPU:1, one launch (start us, length us, event | category | flops | bytes accessed | tf_op | source)
XLA Modules:
  0.0 278.4 jit_solution(14335090463795778304)
XLA Ops:
  0.6 4.5 %collective-permute-start.30 = (f32[1024,1024]{1,0:T(8,128)}, f32[1024,1024]{1,0:T(8,128)}, u32[]{:S(2)}, u32[]{:S(2)}) collective-permute-start(f32[1024,1024]{1,0:T(8,128)} %param.14), channel_id=1, source_target_pairs={{0,1},{1,2},{2,3},{3,4},{4,5},{5,6},{6,7},{7,8},{8,9},{9,10},{10,1... | collective-permute-start | bytes 12582920 | tf_op jit(solution)/shard_map/ppermute | solution.py:26
  5.1 4.9 %fusion.65 = f32[2,64,1024]{2,1,0:T(8,128)S(1)} fusion(f32[2,512,64]{1,2,0:T(8,128)} %param.15, f32[2,512,1024]{2,1,0:T(8,128)} %bitcast.80), kind=kOutput, calls=%fused_computation.138 | convolution fusion | flops 805306368 | bytes 4980736 | tf_op jit(solution)/shard_map/lnr,lnp->lrp/dot_general | solution.py:125
  14.8 38.9 %collective-permute-done.19 = s32[2]{0:T(128)S(1)} collective-permute-done((s32[2]{0:T(128)S(1)}, s32[2]{0:T(128)S(1)}, u32[]{:S(2)}, u32[]{:S(2)}) %collective-permute-start.19) | collective-permute-done | bytes 40 | tf_op jit(solution)/shard_map/ppermute | solution.py:10
  63.4 4.9 %collective-permute-start.24 = (f32[64,128]{1,0:T(8,128)S(1)}, f32[64,128]{1,0:T(8,128)S(1)}, u32[]{:S(2)}, u32[]{:S(2)}) collective-permute-start(f32[64,128]{1,0:T(8,128)S(1)} %select_add_fusion.2), channel_id=1, source_target_pairs={{0,16},{1,17},{2,18},{3,19},{4,20},{5,21},{6,22},{7,23},{8,24},{9,... | collective-permute-start | bytes 98312 | tf_op jit(solution)/shard_map/ppermute | solution.py:16
  68.3 2.2 collective-permute-start.23
  72.6 3.0 %collective-permute-start.17 = (f32[4,64,64]{2,1,0:T(8,128)S(1)}, f32[4,64,64]{2,1,0:T(8,128)S(1)}, u32[]{:S(2)}, u32[]{:S(2)}) collective-permute-start(f32[4,64,64]{2,1,0:T(8,128)S(1)} %maximum_select_fusion.5), channel_id=1, source_target_pairs={{0,4},{1,5},{2,6},{3,7},{4,0},{5,1},{6,2},{7,3},{8,12},{9,13},{10,... | collective-permute-start | bytes 196616 | tf_op jit(solution)/shard_map/ppermute | solution.py:10
  77.3 2.1 collective-permute-done.17
  79.4 6.8 %collective-permute-start.3 = (f32[64,512]{1,0:T(8,128)S(1)}, f32[64,512]{1,0:T(8,128)S(1)}, u32[]{:S(2)}, u32[]{:S(2)}) collective-permute-start(f32[64,512]{1,0:T(8,128)S(1)} %select_add_fusion), channel_id=1, source_target_pairs={{0,14},{1,15},{2,16},{3,17},{4,18},{5,19},{6,20},{7,21},{8,22},{9,... | collective-permute-start | bytes 393224 | tf_op jit(solution)/shard_map/ppermute | solution.py:16
  88.4 46.2 %collective-permute-start.4 = (f32[64,512]{1,0:T(8,128)S(1)}, f32[64,512]{1,0:T(8,128)S(1)}, u32[]{:S(2)}, u32[]{:S(2)}) collective-permute-start(f32[64,512]{1,0:T(8,128)S(1)} %select_add_fusion), channel_id=1, source_target_pairs={{0,12},{1,13},{2,14},{3,15},{4,16},{5,17},{6,18},{7,19},{8,20},{9,... | collective-permute-start | bytes 393224 | tf_op jit(solution)/shard_map/ppermute | solution.py:16
  134.7 2.3 collective-permute-done.4
  140.2 5.7 %collective-permute-start.6 = (f32[64,512]{1,0:T(8,128)S(1)}, f32[64,512]{1,0:T(8,128)S(1)}, u32[]{:S(2)}, u32[]{:S(2)}) collective-permute-start(f32[64,512]{1,0:T(8,128)S(1)} %select_add_fusion), channel_id=1, source_target_pairs={{0,8},{1,9},{2,10},{3,11},{4,12},{5,13},{6,14},{7,15},{8,16},{9,17... | collective-permute-start | bytes 393224 | tf_op jit(solution)/shard_map/ppermute | solution.py:16
  147.8 8.0 %collective-permute-start.7 = (f32[64,512]{1,0:T(8,128)S(1)}, f32[64,512]{1,0:T(8,128)S(1)}, u32[]{:S(2)}, u32[]{:S(2)}) collective-permute-start(f32[64,512]{1,0:T(8,128)S(1)} %select_add_fusion), channel_id=1, source_target_pairs={{0,6},{1,7},{2,8},{3,9},{4,10},{5,11},{6,12},{7,13},{8,14},{9,15},... | collective-permute-start | bytes 393224 | tf_op jit(solution)/shard_map/ppermute | solution.py:16
  162.3 8.0 %collective-permute-done.9 = f32[64,512]{1,0:T(8,128)S(1)} collective-permute-done((f32[64,512]{1,0:T(8,128)S(1)}, f32[64,512]{1,0:T(8,128)S(1)}, u32[]{:S(2)}, u32[]{:S(2)}) %collective-permute-start.9) | collective-permute-done | bytes 131104 | tf_op jit(solution)/shard_map/ppermute | solution.py:16
  171.5 5.7 %collective-permute-done.10 = f32[64,512]{1,0:T(8,128)S(1)} collective-permute-done((f32[64,512]{1,0:T(8,128)S(1)}, f32[64,512]{1,0:T(8,128)S(1)}, u32[]{:S(2)}, u32[]{:S(2)}) %collective-permute-start.10) | collective-permute-done | bytes 131104 | tf_op jit(solution)/shard_map/ppermute | solution.py:16
  178.6 7.1 %collective-permute-done.11 = f32[64,512]{1,0:T(8,128)S(1)} collective-permute-done((f32[64,512]{1,0:T(8,128)S(1)}, f32[64,512]{1,0:T(8,128)S(1)}, u32[]{:S(2)}, u32[]{:S(2)}) %collective-permute-start.11) | collective-permute-done | bytes 131104 | tf_op jit(solution)/shard_map/ppermute | solution.py:16
  186.9 7.7 %collective-permute-done.12 = f32[64,512]{1,0:T(8,128)S(1)} collective-permute-done((f32[64,512]{1,0:T(8,128)S(1)}, f32[64,512]{1,0:T(8,128)S(1)}, u32[]{:S(2)}, u32[]{:S(2)}) %collective-permute-start.12) | collective-permute-done | bytes 131104 | tf_op jit(solution)/shard_map/ppermute | solution.py:16
  196.2 6.9 %collective-permute-done.13 = f32[64,512]{1,0:T(8,128)S(1)} collective-permute-done((f32[64,512]{1,0:T(8,128)S(1)}, f32[64,512]{1,0:T(8,128)S(1)}, u32[]{:S(2)}, u32[]{:S(2)}) %collective-permute-start.13) | collective-permute-done | bytes 131104 | tf_op jit(solution)/shard_map/ppermute | solution.py:16
  203.1 2.7 collective-permute-done.27
  205.8 4.3 %collective-permute-start.28 = (f32[64,256]{1,0:T(8,128)S(1)}, f32[64,256]{1,0:T(8,128)S(1)}, u32[]{:S(2)}, u32[]{:S(2)}) collective-permute-start(f32[64,256]{1,0:T(8,128)S(1)} %maximum_select_fusion.9), channel_id=1, source_target_pairs={{0,2},{1,3},{2,0},{3,1},{4,6},{5,7},{6,4},{7,5},{8,10},{9,11},{10,... | collective-permute-start | bytes 196616 | tf_op jit(solution)/shard_map/ppermute | solution.py:10
  213.4 12.8 %collective-permute-start.29 = (f32[64,512]{1,0:T(8,128)S(1)}, f32[64,512]{1,0:T(8,128)S(1)}, u32[]{:S(2)}, u32[]{:S(2)}) collective-permute-start(f32[64,512]{1,0:T(8,128)S(1)} %fusion.8), channel_id=1, source_target_pairs={{0,1},{1,0},{2,3},{3,2},{4,5},{5,4},{6,7},{7,6},{8,9},{9,8},{10,11... | collective-permute-start | bytes 393224 | tf_op jit(solution)/shard_map/ppermute | solution.py:10
  227.8 5.0 %fusion.66 = f32[2,1024,512]{1,2,0:T(8,128)} fusion(f32[2,64,1024]{2,1,0:T(8,128)S(1)} %convolution_bitcast_fusion, f32[2,512,64]{1,2,0:T(8,128)S(1)} %copy-done.4), kind=kOutput, calls=%fused_computation.139 | convolution fusion | flops 805306368 | bytes 4980736 | tf_op jit(solution)/shard_map/lnr,lrp->lnp/dot_general | solution.py:163
  232.8 7.6 %pad_maximum_fusion = f32[3072,1024]{1,0:T(8,128)} fusion(f32[1024,1024]{1,0:T(8,128)S(1)} %collective-permute-done.31, f32[1024,1024]{1,0:T(8,128)S(1)} %copy-done.3, f32[1024,1024]{1,0:T(8,128)} %collective-permute-done.30), kind=kLoop, calls=%fused_computation.3 | loop fusion | flops 6291456 | bytes 25165824 | tf_op jit(solution)/shard_map/concatenate | solution.py:28
  240.4 11.4 %gather_fusion.2 = f32[6,512,1024]{2,1,0:T(8,128)} fusion(f32[6,512,1024]{2,1,0:T(8,128)} %bitcast.79, s32[1024]{0:T(1024)S(1)} %pad_clamp_fusion), kind=kCustom, calls=%fused_computation.2 | custom fusion | bytes 25165848 | tf_op jit(solution)/shard_map/jit(_take)/gather | solution.py:167
  251.8 26.6 %bitcast_add_fusion = f32[2,1024,512]{1,2,0:T(8,128)} fusion(f32[2,1024,512]{1,2,0:T(8,128)} %fusion.66, f32[2,3,512,512]{3,2,1,0:T(8,128)} %param.24, f32[2,3,512,1024]{3,2,1,0:T(8,128)} %bitcast.78, pred[2,3]{1,0:T(4,128)(4,1)S(1)} %get-tuple-element.5), kind=kOutput, calls=%fused_computation.8 | convolution fusion | flops 19331547136 | bytes 27262982 | tf_op jit(solution)/shard_map/lmab,lmbp->lap/dot_general | solution.py:170
  (114 shorter events, 41.8 us)
Async XLA Ops:
  0.0 53.9 %collective-permute-start.1 = (s32[4]{0:T(128)}, s32[4]{0:T(128)S(1)}, u32[]{:S(2)}, u32[]{:S(2)}) collective-permute-start(s32[4]{0:T(128)} %param.19), channel_id=1, source_target_pairs={{0,1},{1,0},{2,3},{3,2},{4,5},{5,4},{6,7},{7,6},{8,9},{9,8},{10,11... | collective-permute-start | bytes 56 | tf_op jit(solution)/shard_map/ppermute | solution.py:10
  0.1 12.8 %collective-permute-start.18 = (s32[1]{0:T(128)}, s32[1]{0:T(128)}, u32[]{:S(2)}, u32[]{:S(2)}) collective-permute-start(s32[1]{0:T(128)} %param.22), channel_id=1, source_target_pairs={{0,1},{1,0},{2,3},{3,2},{4,5},{5,4},{6,7},{7,6},{8,9},{9,8},{10,11... | collective-permute-start | bytes 20 | tf_op jit(solution)/shard_map/ppermute | solution.py:10
  0.5 58.6 %collective-permute-start.15 = (f32[1,64,64]{2,1,0:T(8,128)}, f32[1,64,64]{2,1,0:T(8,128)S(1)}, u32[]{:S(2)}, u32[]{:S(2)}) collective-permute-start(f32[1,64,64]{2,1,0:T(8,128)} %param.21), channel_id=1, source_target_pairs={{0,1},{1,0},{2,3},{3,2},{4,5},{5,4},{6,7},{7,6},{8,9},{9,8},{10,11... | collective-permute-start | bytes 49160 | tf_op jit(solution)/shard_map/ppermute | solution.py:10
  0.6 232.2 %collective-permute-start.30 = (f32[1024,1024]{1,0:T(8,128)}, f32[1024,1024]{1,0:T(8,128)}, u32[]{:S(2)}, u32[]{:S(2)}) collective-permute-start(f32[1024,1024]{1,0:T(8,128)} %param.14), channel_id=1, source_target_pairs={{0,1},{1,2},{2,3},{3,4},{4,5},{5,6},{6,7},{7,8},{8,9},{9,10},{10,1... | collective-permute-start | bytes 12582920 | tf_op jit(solution)/shard_map/ppermute | solution.py:26
  10.6 43.4 %collective-permute-start.2 = (f32[64,512]{1,0:T(8,128)S(1)}, f32[64,512]{1,0:T(8,128)S(1)}, u32[]{:S(2)}, u32[]{:S(2)}) collective-permute-start(f32[64,512]{1,0:T(8,128)S(1)} %slice_select_fusion), channel_id=1, source_target_pairs={{0,1},{1,0},{2,3},{3,2},{4,5},{5,4},{6,7},{7,6},{8,9},{9,8},{10,11... | collective-permute-start | bytes 393224 | tf_op jit(solution)/shard_map/ppermute | solution.py:10
  13.6 40.2 %collective-permute-start.19 = (s32[2]{0:T(128)S(1)}, s32[2]{0:T(128)S(1)}, u32[]{:S(2)}, u32[]{:S(2)}) collective-permute-start(s32[2]{0:T(128)S(1)} %broadcast_select_fusion), channel_id=1, source_target_pairs={{0,2},{1,3},{2,0},{3,1},{4,6},{5,7},{6,4},{7,5},{8,10},{9,11},{10,... | collective-permute-start | bytes 32 | tf_op jit(solution)/shard_map/ppermute | solution.py:10
  59.1 9.2 %collective-permute-start.16 = (f32[2,64,64]{2,1,0:T(8,128)S(1)}, f32[2,64,64]{2,1,0:T(8,128)S(1)}, u32[]{:S(2)}, u32[]{:S(2)}) collective-permute-start(f32[2,64,64]{2,1,0:T(8,128)S(1)} %maximum_select_fusion.8), channel_id=1, source_target_pairs={{0,2},{1,3},{2,0},{3,1},{4,6},{5,7},{6,4},{7,5},{8,10},{9,11},{10,... | collective-permute-start | bytes 98312 | tf_op jit(solution)/shard_map/ppermute | solution.py:10
  60.8 9.7 %collective-permute-start.26 = (f32[64,128]{1,0:T(8,128)S(1)}, f32[64,128]{1,0:T(8,128)S(1)}, u32[]{:S(2)}, u32[]{:S(2)}) collective-permute-start(f32[64,128]{1,0:T(8,128)S(1)} %select_add_fusion.2), channel_id=1, source_target_pairs={{24,0},{25,1},{26,2},{27,3},{28,4},{29,5},{30,6},{31,7}} | collective-permute-start | bytes 98312 | tf_op jit(solution)/shard_map/ppermute | solution.py:16
  62.1 10.4 %collective-permute-start.25 = (f32[64,128]{1,0:T(8,128)S(1)}, f32[64,128]{1,0:T(8,128)S(1)}, u32[]{:S(2)}, u32[]{:S(2)}) collective-permute-start(f32[64,128]{1,0:T(8,128)S(1)} %select_add_fusion.2), channel_id=1, source_target_pairs={{16,0},{17,1},{18,2},{19,3},{20,4},{21,5},{22,6},{23,7},{24,8},{25... | collective-permute-start | bytes 98312 | tf_op jit(solution)/shard_map/ppermute | solution.py:16
  63.4 9.2 %collective-permute-start.24 = (f32[64,128]{1,0:T(8,128)S(1)}, f32[64,128]{1,0:T(8,128)S(1)}, u32[]{:S(2)}, u32[]{:S(2)}) collective-permute-start(f32[64,128]{1,0:T(8,128)S(1)} %select_add_fusion.2), channel_id=1, source_target_pairs={{0,16},{1,17},{2,18},{3,19},{4,20},{5,21},{6,22},{7,23},{8,24},{9,... | collective-permute-start | bytes 98312 | tf_op jit(solution)/shard_map/ppermute | solution.py:16
  68.3 7.3 %collective-permute-start.23 = (f32[64,128]{1,0:T(8,128)S(1)}, f32[64,128]{1,0:T(8,128)S(1)}, u32[]{:S(2)}, u32[]{:S(2)}) collective-permute-start(f32[64,128]{1,0:T(8,128)S(1)} %select_add_fusion.2), channel_id=1, source_target_pairs={{0,24},{1,25},{2,26},{3,27},{4,28},{5,29},{6,30},{7,31}} | collective-permute-start | bytes 98312 | tf_op jit(solution)/shard_map/ppermute | solution.py:16
  70.5 162.3 %collective-permute-start.31 = (f32[1024,1024]{1,0:T(8,128)}, f32[1024,1024]{1,0:T(8,128)S(1)}, u32[]{:S(2)}, u32[]{:S(2)}) collective-permute-start(f32[1024,1024]{1,0:T(8,128)} %param.14), channel_id=1, source_target_pairs={{1,0},{2,1},{3,2},{4,3},{5,4},{6,5},{7,6},{8,7},{9,8},{10,9},{11,1... | collective-permute-start | bytes 12582920 | tf_op jit(solution)/shard_map/ppermute | solution.py:27
  72.5 139.6 %collective-permute-start = (f32[4,64,64]{2,1,0:T(8,128)S(1)}, f32[4,64,64]{2,1,0:T(8,128)S(1)}, u32[]{:S(2)}, u32[]{:S(2)}) collective-permute-start(f32[4,64,64]{2,1,0:T(8,128)S(1)} %copy-done.6), channel_id=1, source_target_pairs={{0,1},{1,0},{2,3},{3,2},{4,5},{5,4},{6,7},{7,6},{8,9},{9,8},{10,11... | collective-permute-start | bytes 196616 | tf_op jit(solution)/shard_map/ppermute | solution.py:10
  75.6 127.4 %collective-permute-start.14 = (f32[64,512]{1,0:T(8,128)S(1)}, f32[64,512]{1,0:T(8,128)S(1)}, u32[]{:S(2)}, u32[]{:S(2)}) collective-permute-start(f32[64,512]{1,0:T(8,128)S(1)} %select_add_fusion), channel_id=1, source_target_pairs={{14,0},{15,1},{16,2},{17,3},{18,4},{19,5},{20,6},{21,7},{22,8},{23... | collective-permute-start | bytes 393224 | tf_op jit(solution)/shard_map/ppermute | solution.py:16
  79.4 9.0 %collective-permute-start.3 = (f32[64,512]{1,0:T(8,128)S(1)}, f32[64,512]{1,0:T(8,128)S(1)}, u32[]{:S(2)}, u32[]{:S(2)}) collective-permute-start(f32[64,512]{1,0:T(8,128)S(1)} %select_add_fusion), channel_id=1, source_target_pairs={{0,14},{1,15},{2,16},{3,17},{4,18},{5,19},{6,20},{7,21},{8,22},{9,... | collective-permute-start | bytes 393224 | tf_op jit(solution)/shard_map/ppermute | solution.py:16
  88.4 48.6 %collective-permute-start.4 = (f32[64,512]{1,0:T(8,128)S(1)}, f32[64,512]{1,0:T(8,128)S(1)}, u32[]{:S(2)}, u32[]{:S(2)}) collective-permute-start(f32[64,512]{1,0:T(8,128)S(1)} %select_add_fusion), channel_id=1, source_target_pairs={{0,12},{1,13},{2,14},{3,15},{4,16},{5,17},{6,18},{7,19},{8,20},{9,... | collective-permute-start | bytes 393224 | tf_op jit(solution)/shard_map/ppermute | solution.py:16
  140.2 7.6 %collective-permute-start.6 = (f32[64,512]{1,0:T(8,128)S(1)}, f32[64,512]{1,0:T(8,128)S(1)}, u32[]{:S(2)}, u32[]{:S(2)}) collective-permute-start(f32[64,512]{1,0:T(8,128)S(1)} %select_add_fusion), channel_id=1, source_target_pairs={{0,8},{1,9},{2,10},{3,11},{4,12},{5,13},{6,14},{7,15},{8,16},{9,17... | collective-permute-start | bytes 393224 | tf_op jit(solution)/shard_map/ppermute | solution.py:16
  147.8 9.9 %collective-permute-start.7 = (f32[64,512]{1,0:T(8,128)S(1)}, f32[64,512]{1,0:T(8,128)S(1)}, u32[]{:S(2)}, u32[]{:S(2)}) collective-permute-start(f32[64,512]{1,0:T(8,128)S(1)} %select_add_fusion), channel_id=1, source_target_pairs={{0,6},{1,7},{2,8},{3,9},{4,10},{5,11},{6,12},{7,13},{8,14},{9,15},... | collective-permute-start | bytes 393224 | tf_op jit(solution)/shard_map/ppermute | solution.py:16
  161.0 9.3 %collective-permute-start.9 = (f32[64,512]{1,0:T(8,128)S(1)}, f32[64,512]{1,0:T(8,128)S(1)}, u32[]{:S(2)}, u32[]{:S(2)}) collective-permute-start(f32[64,512]{1,0:T(8,128)S(1)} %select_add_fusion), channel_id=1, source_target_pairs={{4,0},{5,1},{6,2},{7,3},{8,4},{9,5},{10,6},{11,7},{12,8},{13,9},{1... | collective-permute-start | bytes 393224 | tf_op jit(solution)/shard_map/ppermute | solution.py:16
  170.2 7.0 %collective-permute-start.10 = (f32[64,512]{1,0:T(8,128)S(1)}, f32[64,512]{1,0:T(8,128)S(1)}, u32[]{:S(2)}, u32[]{:S(2)}) collective-permute-start(f32[64,512]{1,0:T(8,128)S(1)} %select_add_fusion), channel_id=1, source_target_pairs={{6,0},{7,1},{8,2},{9,3},{10,4},{11,5},{12,6},{13,7},{14,8},{15,9},... | collective-permute-start | bytes 393224 | tf_op jit(solution)/shard_map/ppermute | solution.py:16
  177.3 8.4 %collective-permute-start.11 = (f32[64,512]{1,0:T(8,128)S(1)}, f32[64,512]{1,0:T(8,128)S(1)}, u32[]{:S(2)}, u32[]{:S(2)}) collective-permute-start(f32[64,512]{1,0:T(8,128)S(1)} %select_add_fusion), channel_id=1, source_target_pairs={{8,0},{9,1},{10,2},{11,3},{12,4},{13,5},{14,6},{15,7},{16,8},{17,9... | collective-permute-start | bytes 393224 | tf_op jit(solution)/shard_map/ppermute | solution.py:16
  185.6 9.0 %collective-permute-start.12 = (f32[64,512]{1,0:T(8,128)S(1)}, f32[64,512]{1,0:T(8,128)S(1)}, u32[]{:S(2)}, u32[]{:S(2)}) collective-permute-start(f32[64,512]{1,0:T(8,128)S(1)} %select_add_fusion), channel_id=1, source_target_pairs={{10,0},{11,1},{12,2},{13,3},{14,4},{15,5},{16,6},{17,7},{18,8},{19... | collective-permute-start | bytes 393224 | tf_op jit(solution)/shard_map/ppermute | solution.py:16
  194.7 8.4 %collective-permute-start.13 = (f32[64,512]{1,0:T(8,128)S(1)}, f32[64,512]{1,0:T(8,128)S(1)}, u32[]{:S(2)}, u32[]{:S(2)}) collective-permute-start(f32[64,512]{1,0:T(8,128)S(1)} %select_add_fusion), channel_id=1, source_target_pairs={{12,0},{13,1},{14,2},{15,3},{16,4},{17,5},{18,6},{19,7},{20,8},{21... | collective-permute-start | bytes 393224 | tf_op jit(solution)/shard_map/ppermute | solution.py:16
  213.4 13.8 %collective-permute-start.29 = (f32[64,512]{1,0:T(8,128)S(1)}, f32[64,512]{1,0:T(8,128)S(1)}, u32[]{:S(2)}, u32[]{:S(2)}) collective-permute-start(f32[64,512]{1,0:T(8,128)S(1)} %fusion.8), channel_id=1, source_target_pairs={{0,1},{1,0},{2,3},{3,2},{4,5},{5,4},{6,7},{7,6},{8,9},{9,8},{10,11... | collective-permute-start | bytes 393224 | tf_op jit(solution)/shard_map/ppermute | solution.py:10
  (20 other events, 480.8 us)
where the time goes:
time: 279 us; the launch traced here: 278 us
  starting transfers between devices  119 us (43%)
  waiting for transfers between devices  94.5 us (34%)
  matrix products  42 us (15%)
  local copies, waits for them, and re-layouts  12.9 us (5%)
  other arithmetic  8.78 us (3%)
    ppermute x16, starting transfers between devices, shifted(): return lax.ppermute(shard, axis, pairs)  86.7 us
    ppermute x14, waiting for transfers between devices, swapped(): lax.ppermute(shard, axis, [(i, i ^ 1 << apart) for i in range(lax.axis_si...  47.3 us
    ppermute x16, waiting for transfers between devices, shifted(): return lax.ppermute(shard, axis, pairs)  47.1 us
    dot_general x1, matrix products, body(): jnp.einsum('lmab,lmbp->lap', near_blocks, near_rows, precision=highest)  26.6 us
    ppermute x14, starting transfers between devices, swapped(): lax.ppermute(shard, axis, [(i, i ^ 1 << apart) for i in range(lax.axis_si...  25.8 us
    gather x1, local copies, waits for them, and re-layouts, body(): jnp.take(padded, local_index.reshape(-1), axis=0)  11.4 us
    concatenate x1, other arithmetic, padded_2(): shard = jnp.concatenate([before, shard, after], axis=dim)  7.57 us
  transfers between devices with their start and end apart: 32, of which 17 were waited for; matrix products, arithmetic and copies ran while one was open for 6% of the time, Pallas kernels for 0%

commit v1 on v0

v1 whole, which is shorter than its diff:
```python
import functools

import jax
import jax.numpy as jnp
from jax import lax
from jax.experimental import pallas as pl
from jax.experimental.pallas import tpu as pltpu
from jax.sharding import PartitionSpec as P

MESH = pl.DeviceIdType.MESH
GROUP = 4
LANES = 128
partner_offsets = (-7, -6, -5, -4, -3, -2, 2, 3, 4, 5, 6, 7)


def split(x):
    high = x.astype(jnp.bfloat16)
    low = (x - high.astype(jnp.float32)).astype(jnp.bfloat16)
    return high, low


def dot_split(a, b):
    one = functools.partial(jnp.dot, preferred_element_type=jnp.float32)
    return one(a[0], b[0]) + (one(a[0], b[1]) + one(a[1], b[0]))


def dot(a, b):
    return dot_split(split(a), split(b))


def kernel(
    devices,
    offsets,
    probes,
    basis,
    transfer,
    cluster,
    cone,
    pone,
    none,
    ctwo,
    ptwo,
    ntwo,
    near,
    nlist,
    out,
    *scratch,
):
    chunks = len(scratch) - 19
    bufs = scratch[:chunks]
    (near_f, near_h, near_l, total, part, half, share, coef, own_two, two, packed, down, dn, lift,
     send, recv, halo_send, halo_recv, near_sem) = scratch[chunks:]
    leaves, size, rank = basis.shape
    wide = bufs[0].shape[2]
    per_chunk = wide // LANES
    me = lax.axis_index("leaf")
    plane_size = GROUP * 2
    planes = devices // plane_size
    q = lax.div(me, plane_size)
    r = lax.rem(me, plane_size)
    core = lax.rem(r, 2)
    c4 = lax.div(r, 2)
    mate = me + 1 - 2 * core
    beside = me - 1 + 2 * core
    has_beside = (beside >= 0) & (beside < devices)

    def chip(t):
        return q * plane_size + t * 2 + core

    def xor(value, bits):
        result = value
        for bit in (1, 2):
            if bits & bit:
                result = result + bit - 2 * bit * lax.rem(lax.div(value, bit), 2)
        return result

    def reaches(o):
        other = q + o
        apart = lax.div(other + 8, GROUP) - lax.div(q + 8, GROUP)
        return (other >= 0) & (other < planes) & (apart <= 1) & (apart >= -1)

    def remote(src, dst, ss, rs, device):
        return pltpu.make_async_remote_copy(
            src_ref=src, dst_ref=dst, send_sem=ss, recv_sem=rs,
            device_id=(device,), device_id_type=MESH,
        )

    def go(index, src, dst, device):
        return remote(src, dst, send.at[index], recv.at[index], device)

    barrier = pltpu.get_barrier_semaphore()

    def greet(device):
        pl.semaphore_signal(barrier, inc=1, device_id=(device,), device_id_type=MESH)

    greet(mate)
    for s in (1, 2, 3):
        greet(chip(xor(c4, s)))
    maybe = [(has_beside, beside), (q > 0, me - plane_size), (q < planes - 1, me + plane_size)]
    maybe += [(reaches(o), me + o * plane_size) for o in offsets]
    expected = jnp.int32(4)
    for there, device in maybe:
        pl.when(there)(functools.partial(greet, device))
        expected = expected + jnp.where(there, 1, 0)
    pl.semaphore_wait(barrier, expected)

    def halo(k, far):
        src = probes.at[:, :, pl.ds(k * wide, wide)]
        if far:
            dst = bufs[k].at[pl.ds((1 - core) * 2 * leaves, leaves)]
            return remote(src, dst, halo_send.at[0, k], halo_recv.at[0, k], beside)
        dst = bufs[k].at[pl.ds(core * 2 * leaves, leaves)]
        return remote(src, dst, halo_send.at[1, k], halo_recv.at[1, k], mate)

    own_copies = [
        pltpu.make_async_copy(
            probes.at[:, :, pl.ds(k * wide, wide)],
            bufs[k].at[pl.ds(leaves, leaves)],
            near_sem.at[k],
        )
        for k in range(chunks)
    ]
    near_copy = pltpu.make_async_copy(near, near_f, near_sem.at[chunks])
    for copy in own_copies:
        copy.start()

    for k in range(chunks):
        pl.when(has_beside)(halo(k, True).start)
    for k in range(chunks):
        halo(k, False).start()

    near_copy.start()

    slot = core * GROUP + c4
    slots = cone.shape[0]
    for s in range(slots // 2):
        packed[slot, pl.ds(s * rank, rank), :] = jnp.concatenate(
            [cone[2 * s], cone[2 * s + 1]], axis=1
        )
    packed[slot, pl.ds(slots // 2 * rank, rank), :] = jnp.concatenate([ctwo[0], ctwo[0]], axis=1)
    mine = q * GROUP + c4
    ids = [
        jnp.where(core * slots + k < none[mine], pone[k], -1) for k in range(slots)
    ]
    ids.append(jnp.where(r < ntwo[q], ptwo[0], -1))
    row = lax.broadcasted_iota(jnp.int32, (8, LANES), 0)
    table = jnp.full((8, LANES), -1, jnp.int32)
    for k, value in enumerate(ids):
        table = jnp.where(row == k, value, table)
    id_row = slots // 2 * rank + rank
    packed[slot, pl.ds(id_row, 8), :] = table.astype(jnp.float32)
    bit_x, bit_y = lax.rem(c4, 2), lax.div(c4, 2)
    pack_x = go(6, packed.at[pl.ds(slot, 1)], packed.at[pl.ds(slot, 1)], chip(xor(c4, 1)))
    pair = core * GROUP + bit_y * 2
    pack_y = go(7, packed.at[pl.ds(pair, 2)], packed.at[pl.ds(pair, 2)], chip(xor(c4, 2)))
    quad = core * GROUP
    pack_c = go(8, packed.at[pl.ds(quad, 4)], packed.at[pl.ds(quad, 4)], mate)
    pack_x.start()

    for l in range(leaves):
        lift[l] = dot(basis[l], transfer[l])
    lifts = [split(lift[l].T) for l in range(leaves)]
    for k in range(chunks):
        own_copies[k].wait()
        value = sum(
            dot_split(lifts[l], split(bufs[k][leaves + l]))
            for l in range(leaves)
        )
        for g in range(per_chunk):
            part[k * per_chunk + g] = value[:, g * LANES:(g + 1) * LANES]
    halve = go(0, part.at[pl.ds((1 - core) * GROUP, GROUP)], half, mate)
    halve.start()
    pack_x.wait_recv()
    pack_y.start()
    halve.wait_recv()
    for t in range(GROUP):
        share[t] = part[core * GROUP + t] + half[t]
    spread = [
        go(s, share.at[xor(c4, s)], coef.at[GROUP + c4], chip(xor(c4, s))) for s in (1, 2, 3)
    ]
    for copy in spread:
        copy.start()
    coef[GROUP + c4] = share[c4]
    pack_y.wait_recv()
    pack_c.start()

    def near_split(index, _):
        l, m = lax.div(index, near.shape[1]), lax.rem(index, near.shape[1])
        near_h[l, m], near_l[l, m] = split(near_f[l, m])
        return _

    near_copy.wait()
    lax.fori_loop(0, leaves * near.shape[1], near_split, 0)

    for copy in spread:
        copy.wait_recv()
    up = go(4, coef.at[pl.ds(GROUP, GROUP)], coef.at[pl.ds(0, GROUP)], me + plane_size)
    lower = go(5, coef.at[pl.ds(GROUP, GROUP)], coef.at[pl.ds(2 * GROUP, GROUP)], me - plane_size)
    pl.when(q < planes - 1)(up.start)
    pl.when(q > 0)(lower.start)
    own_two[...] = sum(
        dot(cluster[q * GROUP + j].T, coef[GROUP + j]) for j in range(GROUP)
    )
    two_copies = []
    for i, o in enumerate(offsets):
        copy = go(13 + i, own_two, two.at[offsets.index(-o)], me + o * plane_size)
        two_copies.append((o, copy))
        pl.when(reaches(o))(copy.start)

    def own_near(l, _):
        at = pl.ds(pl.multiple_of(l * size, size), size)
        for k in range(chunks):
            x = bufs[k][leaves + l]
            total[at, k * wide:(k + 1) * wide] = dot_split((near_h[l, 0], near_l[l, 0]), split(x))
        return _

    lax.fori_loop(0, leaves, own_near, 0)

    pl.when(q > 0)(up.wait_recv)
    pl.when(q < planes - 1)(lower.wait_recv)
    for o, copy in two_copies:
        pl.when(reaches(-o))(copy.wait_recv)
    pack_c.wait_recv()

    zero = jnp.zeros((rank, LANES), jnp.float32)

    def chosen(at, k, options):
        picked = zero
        label = packed[at, pl.ds(id_row + k, 1), :]
        for number, value in options:
            picked = jnp.where(label == number.astype(jnp.float32), value, picked)
        return picked

    far_two = zero
    for at in range(plane_size):
        options = [(q + o, two[i]) for i, o in enumerate(offsets)]
        far_two += dot(
            packed[at, pl.ds(slots // 2 * rank, rank), :][:, :rank], chosen(at, slots, options)
        )

    far_two_split = split(far_two)

    def cluster_far(j, _):
        value = dot_split(split(cluster[q * GROUP + j]), far_two_split)
        options = [((q - 1) * GROUP + i, coef[i]) for i in range(3 * GROUP)]
        for k in range(2):
            at = k * GROUP + j
            for s in range(slots // 2):
                partner = jnp.concatenate(
                    [chosen(at, 2 * s, options), chosen(at, 2 * s + 1, options)], axis=0
                )
                value += dot(packed[at, pl.ds(s * rank, rank), :], partner)
        down[j] = value
        return _

    lax.fori_loop(0, GROUP, cluster_far, 0)
    mine_at = core * GROUP + c4
    back = [
        go(8 + s, down.at[xor(c4, s)], dn.at[mine_at], chip(xor(c4, s))) for s in (1, 2, 3)
    ]
    for copy in back:
        copy.start()
    dn[mine_at] = down[c4]
    for copy in back:
        copy.wait_recv()
    join = go(12, dn.at[pl.ds(quad, 4)], dn.at[pl.ds(quad, 4)], mate)
    join.start()
    join.wait_recv()

    def far_rows(l, _):
        at = pl.ds(pl.multiple_of(l * size, size), size)
        tall = split(lift[l])
        for k in range(chunks):
            value = jnp.concatenate(
                [dn[k * per_chunk + g] for g in range(per_chunk)], axis=1
            )
            total[at, k * wide:(k + 1) * wide] += dot_split(tall, split(value))
        return _

    lax.fori_loop(0, leaves, far_rows, 0)

    results = []
    for k in range(chunks):
        halo(k, False).wait_recv()
        pl.when(has_beside)(halo(k, True).wait_recv)

        def other_near(l, _, k=k):
            at = pl.ds(pl.multiple_of(l * size, size), size)
            value = total[at, k * wide:(k + 1) * wide]
            for m in range(1, near.shape[1]):
                index = nlist[l, m] - (me - 1) * leaves
                index = jnp.maximum(0, jnp.minimum(index, 3 * leaves - 1))
                value += dot_split((near_h[l, m], near_l[l, m]), split(bufs[k][index]))
            total[at, k * wide:(k + 1) * wide] = value
            return _

        lax.fori_loop(0, leaves, other_near, 0)
        copy = pltpu.make_async_copy(
            total.at[:, pl.ds(k * wide, wide)],
            out.at[:, pl.ds(k * wide, wide)],
            near_sem.at[k],
        )
        copy.start()
        results.append(copy)

    for copy in [halve, pack_x, pack_y, pack_c, join] + spread + back:
        copy.wait_send()
    pl.when(q < planes - 1)(up.wait_send)
    pl.when(q > 0)(lower.wait_send)
    for o, copy in two_copies:
        pl.when(reaches(o))(copy.wait_send)
    for k in range(chunks):
        halo(k, False).wait_send()
        pl.when(has_beside)(halo(k, True).wait_send)
    for copy in results:
        copy.wait()


def body(devices, *args):
    probes, basis, near = args[0], args[1], args[10]
    slots = args[4].shape[0]
    leaves, size, rank = basis.shape
    rows, width = probes.shape
    planes = devices // (2 * GROUP)
    offsets = tuple(o for o in partner_offsets if abs(o) < planes)
    chunks = 4
    groups = width // LANES
    wide = width // chunks
    assert leaves == 2 and groups == 2 * GROUP and 2 * rank == LANES
    vmem = pl.BlockSpec(memory_space=pltpu.VMEM)
    smem = pl.BlockSpec(memory_space=pltpu.SMEM)
    anywhere = pl.BlockSpec(memory_space=pl.ANY)
    f32, bf16 = jnp.float32, jnp.bfloat16
    small = lambda n: pltpu.VMEM((n, rank, LANES), f32)
    dma = pltpu.SemaphoreType.DMA
    flops = 2 * (near.size + 2 * basis.size) * width
    return pl.pallas_call(
        functools.partial(kernel, devices, offsets),
        out_shape=jax.ShapeDtypeStruct((rows, width), f32),
        in_specs=[anywhere, vmem, vmem, vmem, vmem, smem, smem, vmem, smem, smem, anywhere, smem],
        out_specs=anywhere,
        scratch_shapes=[pltpu.VMEM((3 * leaves, size, wide), f32)] * chunks
        + [
            pltpu.VMEM(near.shape, f32),
            pltpu.VMEM(near.shape, bf16),
            pltpu.VMEM(near.shape, bf16),
            pltpu.VMEM((rows, width), f32),
            small(groups),
            small(GROUP),
            small(GROUP),
            small(3 * GROUP),
            pltpu.VMEM((rank, LANES), f32),
            small(max(1, len(offsets))),
            pltpu.VMEM((2 * GROUP, (slots // 2 + 1) * rank + 8, LANES), f32),
            small(GROUP),
            small(groups),
            pltpu.VMEM((leaves, size, rank), f32),
            dma((13 + len(offsets),)),
            dma((13 + len(offsets),)),
            dma((2, chunks)),
            dma((2, chunks)),
            dma((chunks + 1,)),
        ],
        compiler_params=pltpu.CompilerParams(
            collective_id=0, has_side_effects=True, vmem_limit_bytes=52 * 1024 * 1024
        ),
        cost_estimate=pl.CostEstimate(
            flops=3 * flops, bytes_accessed=4 * (near.size + 4 * probes.size), transcendentals=0
        ),
    )(probes.reshape(leaves, size, width), *args[1:])


def solution(mesh):
    return jax.shard_map(
        functools.partial(body, mesh.shape["leaf"]),
        mesh=mesh,
        in_specs=(
            P("leaf", None),
            P("leaf", None, None),
            P("leaf", None, None),
            P(),
            P("leaf", None, None),
            P("leaf"),
            P(),
            P("leaf", None, None),
            P("leaf"),
            P(),
            P("leaf", None, None, None),
            P("leaf", None),
        ),
        out_specs=P("leaf", None),
        check_vma=False,
    )
```

time: 279 us -> 143 us (0.51)
  Pallas kernels: 0 us -> 130 us
  starting transfers between devices: 119 us -> 0 us
  waiting for transfers between devices: 94.5 us -> 0 us
  matrix products: 42 us -> 0 us
  other arithmetic: 8.78 us -> 0 us
    pallas_call x0 -> x1, Pallas kernels: none -> 130 us  [body(): pl.pallas_call(functools.partial(kernel, devices, offsets), out_shape=jax...]
    ppermute x32 -> x0, starting transfers between devices: 119 us -> none  [the longest x16 86.7 us: shifted(): return lax.ppermute(shard, axis, pairs)]
    ppermute x32 -> x0, waiting for transfers between devices: 94.5 us -> none  [the longest x14 47.3 us: swapped(): lax.ppermute(shard, axis, [(i, i ^ 1 << apart) for i in range(lax.axis_si...]
    dot_general x11 -> x0, matrix products: 42 us -> none  [the longest x1 26.6 us: body(): jnp.einsum('lmab,lmbp->lap', near_blocks, near_rows, precision=highest)]
    gather x3 -> x0, local copies, waits for them, and re-layouts: 12.6 us -> none  [the longest x1 11.4 us: body(): jnp.take(padded, local_index.reshape(-1), axis=0)]
    unnamed x35 -> x18, local copies, waits for them, and re-layouts: 0.19 us -> 12.1 us
    concatenate x1 -> x0, other arithmetic: 7.57 us -> none  [padded_2(): shard = jnp.concatenate([before, shard, after], axis=dim)]
  transfers between devices with their start and end apart: 32 -> 0, of which waited for: 17 -> 0; matrix products, arithmetic and copies ran while one was open for 6% -> 0% of each run, Pallas kernels for 0% -> 0%
where the time goes in v1:
time: 143 us
  Pallas kernels  130 us (91%)
  local copies, waits for them, and re-layouts  12.1 us (8%)
    pallas_call x1, Pallas kernels, body(): pl.pallas_call(functools.partial(kernel, devices, offsets), out_shape=jax...  130 us
    unnamed x18, local copies, waits for them, and re-layouts  12.1 us

profile of v1, /device:TPU:1, one launch (start us, length us, event | category | flops | bytes accessed | tf_op | source)
XLA Modules:
  0.0 142.6 jit_solution(15344072941048652276)
XLA Ops:
  0.7 1.1 copy.13.basis
  1.8 0.0 copy-start
  1.8 1.0 copy-done
  2.9 0.0 copy-start.1
  2.9 0.9 copy-done.1
  3.8 0.0 copy-start.2
  3.8 0.8 copy-done.2
  4.6 0.0 copy-start.3
  4.6 0.8 copy-done.3
  5.4 0.0 copy-start.4
  5.4 0.7 copy-done.4
  6.0 0.0 copy-start.5
  6.0 0.7 copy-done.5
  6.7 0.0 copy-start.6
  6.7 0.7 copy-done.6
  7.3 0.0 copy-start.7
  7.3 0.7 copy-done.7
  8.0 129.8 %shard_map.118 = f32[1024,1024]{1,0:T(8,128)} custom-call(f32[2,512,1024]{2,1,0:T(8,128)} %bitcast.1, f32[2,512,64]{2,1,0:T(8,128)S(1)} %copy.13.basis, f32[2,64,64]{2,1,0:T(8,128)S(1)} %copy-done.2, f32[16,64,64]{2,1,0:T(8,128)S(1)} %copy-done, f32[4,64,64]{2,1,0:T(8,128)S(1)} %copy-done.1, s32[4]{0:T(128)S(1)} %copy-done.5, s32[16]{0:T(128)S(1)} %copy-done.6, ...), custom_call_target="tpu_custom_call" | custom-call | flops 10468982784 | bytes 23068672 | tf_op jit(solution)/shard_map/pallas_call | solution.py:337
  137.8 4.8 %copy.16 = f32[1024,1024]{1,0:T(8,128)} copy(f32[1024,1024]{1,0:T(8,128)} %shard_map.118) | data formatting | bytes 8388608
Async XLA Ops:
  1.8 1.0 copy-start
  2.9 0.9 copy-start.1
  3.8 0.8 copy-start.2
  4.6 0.8 copy-start.3
  5.4 0.7 copy-start.4
  6.0 0.7 copy-start.5
  6.7 0.7 copy-start.6
  7.3 0.7 copy-start.7

commit v2 on v1

--- a/solution.py
+++ b/solution.py
@@ -32,25 +32,26 @@
     devices,
     offsets,
     probes,
-    basis,
-    transfer,
-    cluster,
-    cone,
-    pone,
-    none,
-    ctwo,
+    basis_hbm,
+    transfer_hbm,
+    cluster_hbm,
+    cone_hbm,
+    pone_hbm,
+    none_hbm,
+    ctwo_hbm,
     ptwo,
-    ntwo,
+    ntwo_hbm,
     near,
-    nlist,
+    nlist_hbm,
     out,
     *scratch,
 ):
-    chunks = len(scratch) - 19
+    chunks = len(scratch) - 29
     bufs = scratch[:chunks]
-    (near_f, near_h, near_l, total, part, half, share, coef, own_two, two, packed, down, dn, lift,
+    (basis, transfer, cluster, cone, pone, none, ctwo, ntwo, nlist, small_sem,
+     near_f, near_h, near_l, total, part, half, share, coef, own_two, two, packed, down, dn, lift,
      send, recv, halo_send, halo_recv, near_sem) = scratch[chunks:]
-    leaves, size, rank = basis.shape
+    leaves, rank, size = basis.shape
     wide = bufs[0].shape[2]
     per_chunk = wide // LANES
     me = lax.axis_index("leaf")
@@ -88,6 +89,27 @@
     def go(index, src, dst, device):
         return remote(src, dst, send.at[index], recv.at[index], device)
 
+    own_copies = [
+        pltpu.make_async_copy(
+            probes.at[:, :, pl.ds(k * wide, wide)],
+            bufs[k].at[pl.ds(leaves, leaves)],
+            near_sem.at[k],
+        )
+        for k in range(chunks)
+    ]
+    near_copy = pltpu.make_async_copy(near, near_f, near_sem.at[chunks])
+    plane_clusters = cluster_hbm.at[pl.ds(q * GROUP, GROUP)]
+    small_copies = [
+        pltpu.make_async_copy(a, b, small_sem.at[i])
+        for i, (a, b) in enumerate((
+            (basis_hbm, basis), (transfer_hbm, transfer), (cone_hbm, cone), (ctwo_hbm, ctwo),
+            (pone_hbm, pone), (none_hbm, none), (ntwo_hbm, ntwo),
+            (plane_clusters, cluster), (nlist_hbm, nlist),
+        ))
+    ]
+    for copy in small_copies[:2] + own_copies + small_copies[2:]:
+        copy.start()
+
     barrier = pltpu.get_barrier_semaphore()
 
     def greet(device):
@@ -104,33 +126,41 @@
         expected = expected + jnp.where(there, 1, 0)
     pl.semaphore_wait(barrier, expected)
 
-    def halo(k, far):
+    def halo(k, far, l=0):
+        if far:
+            src = probes.at[pl.ds(l, 1), :, pl.ds(k * wide, wide)]
+            dst = bufs[k].at[pl.ds((1 - core) * 2 * leaves + l, 1)]
+            return remote(src, dst, halo_send.at[l, k], halo_recv.at[l, k], beside)
         src = probes.at[:, :, pl.ds(k * wide, wide)]
-        if far:
-            dst = bufs[k].at[pl.ds((1 - core) * 2 * leaves, leaves)]
-            return remote(src, dst, halo_send.at[0, k], halo_recv.at[0, k], beside)
         dst = bufs[k].at[pl.ds(core * 2 * leaves, leaves)]
-        return remote(src, dst, halo_send.at[1, k], halo_recv.at[1, k], mate)
-
-    own_copies = [
-        pltpu.make_async_copy(
-            probes.at[:, :, pl.ds(k * wide, wide)],
-            bufs[k].at[pl.ds(leaves, leaves)],
-            near_sem.at[k],
-        )
-        for k in range(chunks)
-    ]
-    near_copy = pltpu.make_async_copy(near, near_f, near_sem.at[chunks])
-    for copy in own_copies:
-        copy.start()
-
+        return remote(src, dst, halo_send.at[leaves, k], halo_recv.at[leaves, k], mate)
+
+    def piece(p):
+        pl.when(has_beside)(halo(p // leaves, True, p % leaves).start)
+
+    piece(0)
+    piece(1)
+    near_copy.start()
+
+    for copy in small_copies[:2]:
+        copy.wait()
+    flat = [dot(transfer[l].T, basis[l]) for l in range(leaves)]
+    lifts = [split(value) for value in flat]
+    for l in range(leaves):
+        lift[l] = flat[l].T
     for k in range(chunks):
-        pl.when(has_beside)(halo(k, True).start)
-    for k in range(chunks):
-        halo(k, False).start()
-
-    near_copy.start()
-
+        own_copies[k].wait()
+        value = sum(
+            dot_split(lifts[l], split(bufs[k][leaves + l]))
+            for l in range(leaves)
+        )
+        for g in range(per_chunk):
+            part[k * per_chunk + g] = value[:, g * LANES:(g + 1) * LANES]
+    halve = go(0, part.at[pl.ds((1 - core) * GROUP, GROUP)], half, mate)
+    halve.start()
+
+    for copy in small_copies[2:]:
+        copy.wait()
     slot = core * GROUP + c4
     slots = cone.shape[0]
     for s in range(slots // 2):
@@ -156,22 +186,6 @@
     quad = core * GROUP
     pack_c = go(8, packed.at[pl.ds(quad, 4)], packed.at[pl.ds(quad, 4)], mate)
     pack_x.start()
-
-    for l in range(leaves):
-        lift[l] = dot(basis[l], transfer[l])
-    lifts = [split(lift[l].T) for l in range(leaves)]
-    for k in range(chunks):
-        own_copies[k].wait()
-        value = sum(
-            dot_split(lifts[l], split(bufs[k][leaves + l]))
-            for l in range(leaves)
-        )
-        for g in range(per_chunk):
-            part[k * per_chunk + g] = value[:, g * LANES:(g + 1) * LANES]
-    halve = go(0, part.at[pl.ds((1 - core) * GROUP, GROUP)], half, mate)
-    halve.start()
-    pack_x.wait_recv()
-    pack_y.start()
     halve.wait_recv()
     for t in range(GROUP):
         share[t] = part[core * GROUP + t] + half[t]
@@ -181,8 +195,10 @@
     for copy in spread:
         copy.start()
     coef[GROUP + c4] = share[c4]
-    pack_y.wait_recv()
-    pack_c.start()
+    piece(2)
+    halo(0, False).start()
+    pack_x.wait_recv()
+    pack_y.start()
 
     def near_split(index, _):
         l, m = lax.div(index, near.shape[1]), lax.rem(index, near.shape[1])
@@ -199,13 +215,18 @@
     pl.when(q < planes - 1)(up.start)
     pl.when(q > 0)(lower.start)
     own_two[...] = sum(
-        dot(cluster[q * GROUP + j].T, coef[GROUP + j]) for j in range(GROUP)
+        dot(cluster[j].T, coef[GROUP + j]) for j in range(GROUP)
     )
     two_copies = []
     for i, o in enumerate(offsets):
         copy = go(13 + i, own_two, two.at[offsets.index(-o)], me + o * plane_size)
         two_copies.append((o, copy))
         pl.when(reaches(o))(copy.start)
+    piece(3)
+    piece(4)
+    halo(1, False).start()
+    pack_y.wait_recv()
+    pack_c.start()
 
     def own_near(l, _):
         at = pl.ds(pl.multiple_of(l * size, size), size)
@@ -241,7 +262,7 @@
     far_two_split = split(far_two)
 
     def cluster_far(j, _):
-        value = dot_split(split(cluster[q * GROUP + j]), far_two_split)
+        value = dot_split(split(cluster[j]), far_two_split)
         options = [((q - 1) * GROUP + i, coef[i]) for i in range(3 * GROUP)]
         for k in range(2):
             at = k * GROUP + j
@@ -260,11 +281,17 @@
     ]
     for copy in back:
         copy.start()
+    piece(5)
+    halo(2, False).start()
     dn[mine_at] = down[c4]
     for copy in back:
         copy.wait_recv()
     join = go(12, dn.at[pl.ds(quad, 4)], dn.at[pl.ds(quad, 4)], mate)
     join.start()
+    for p in range(6, chunks * leaves):
+        piece(p)
+    for k in range(3, chunks):
+        halo(k, False).start()
     join.wait_recv()
 
     def far_rows(l, _):
@@ -282,7 +309,8 @@
     results = []
     for k in range(chunks):
         halo(k, False).wait_recv()
-        pl.when(has_beside)(halo(k, True).wait_recv)
+        for l in range(leaves):
+            pl.when(has_beside)(halo(k, True, l).wait_recv)
 
         def other_near(l, _, k=k):
             at = pl.ds(pl.multiple_of(l * size, size), size)
@@ -311,7 +339,8 @@
         pl.when(reaches(o))(copy.wait_send)
     for k in range(chunks):
         halo(k, False).wait_send()
-        pl.when(has_beside)(halo(k, True).wait_send)
+        for l in range(leaves):
+            pl.when(has_beside)(halo(k, True, l).wait_send)
     for copy in results:
         copy.wait()
 
@@ -327,9 +356,8 @@
     groups = width // LANES
     wide = width // chunks
     assert leaves == 2 and groups == 2 * GROUP and 2 * rank == LANES
-    vmem = pl.BlockSpec(memory_space=pltpu.VMEM)
     smem = pl.BlockSpec(memory_space=pltpu.SMEM)
-    anywhere = pl.BlockSpec(memory_space=pl.ANY)
+    anywhere = pl.BlockSpec(memory_space=pltpu.HBM)
     f32, bf16 = jnp.float32, jnp.bfloat16
     small = lambda n: pltpu.VMEM((n, rank, LANES), f32)
     dma = pltpu.SemaphoreType.DMA
@@ -337,10 +365,20 @@
     return pl.pallas_call(
         functools.partial(kernel, devices, offsets),
         out_shape=jax.ShapeDtypeStruct((rows, width), f32),
-        in_specs=[anywhere, vmem, vmem, vmem, vmem, smem, smem, vmem, smem, smem, anywhere, smem],
+        in_specs=[anywhere] * 8 + [smem] + [anywhere] * (len(args) - 9),
         out_specs=anywhere,
         scratch_shapes=[pltpu.VMEM((3 * leaves, size, wide), f32)] * chunks
         + [
+            pltpu.VMEM((leaves, rank, size), f32),
+            pltpu.VMEM(args[2].shape, f32),
+            pltpu.VMEM((GROUP, rank, rank), f32),
+            pltpu.VMEM(args[4].shape, f32),
+            pltpu.SMEM(args[5].shape, jnp.int32),
+            pltpu.SMEM(args[6].shape, jnp.int32),
+            pltpu.VMEM(args[7].shape, f32),
+            pltpu.SMEM(args[9].shape, jnp.int32),
+            pltpu.SMEM(args[11].shape, jnp.int32),
+            dma((9,)),
             pltpu.VMEM(near.shape, f32),
             pltpu.VMEM(near.shape, bf16),
             pltpu.VMEM(near.shape, bf16),
@@ -357,17 +395,17 @@
             pltpu.VMEM((leaves, size, rank), f32),
             dma((13 + len(offsets),)),
             dma((13 + len(offsets),)),
-            dma((2, chunks)),
-            dma((2, chunks)),
+            dma((leaves + 1, chunks)),
+            dma((leaves + 1, chunks)),
             dma((chunks + 1,)),
         ],
         compiler_params=pltpu.CompilerParams(
-            collective_id=0, has_side_effects=True, vmem_limit_bytes=52 * 1024 * 1024
+            collective_id=0, has_side_effects=True, vmem_limit_bytes=64 * 1024 * 1024 - 64 * 1024
         ),
         cost_estimate=pl.CostEstimate(
             flops=3 * flops, bytes_accessed=4 * (near.size + 4 * probes.size), transcendentals=0
         ),
-    )(probes.reshape(leaves, size, width), *args[1:])
+    )(probes.reshape(leaves, size, width), jnp.swapaxes(basis, 1, 2), *args[2:])
 
 
 def solution(mesh):

time: 143 us -> 111 us (0.78)
  Pallas kernels: 130 us -> 105 us
  local copies, waits for them, and re-layouts: 12.1 us -> 4.79 us
    pallas_call x1, Pallas kernels: 130 us -> 105 us  [body(): pl.pallas_call(functools.partial(kernel, devices, offsets), out_shape=jax...]
    unnamed x18 -> x1, local copies, waits for them, and re-layouts: 12.1 us -> 4.79 us
where the time goes in v2:
time: 111 us
  Pallas kernels  105 us (95%)
  local copies, waits for them, and re-layouts  4.79 us (4%)
    pallas_call x1, Pallas kernels, body(): pl.pallas_call(functools.partial(kernel, devices, offsets), out_shape=jax...  105 us
    unnamed x1, local copies, waits for them, and re-layouts  4.79 us

profile of v2, /device:TPU:1, one launch (start us, length us, event | category | flops | bytes accessed | tf_op | source)
XLA Modules:
  0.0 110.6 jit_solution(7871175524248592932)
XLA Ops:
  0.7 105.2 %shard_map.118 = f32[1024,1024]{1,0:T(8,128)} custom-call(f32[2,512,1024]{2,1,0:T(8,128)} %bitcast.2, f32[2,64,512]{2,1,0:T(8,128)} %bitcast.3, f32[2,64,64]{2,1,0:T(8,128)} %transfer_hbm.1, f32[16,64,64]{2,1,0:T(8,128)} %cluster_hbm.1, f32[4,64,64]{2,1,0:T(8,128)} %cone_hbm.1, s32[4]{0:T(128)} %pone_hbm.1, s32[16]{0:T(128)} %none_hbm.1, ...), custom_call_target="tpu_custom_call" | custom-call | flops 10468982784 | bytes 23068672 | tf_op jit(solution)/shard_map/pallas_call | solution.py:365
  105.8 4.8 %copy.15 = f32[1024,1024]{1,0:T(8,128)} copy(f32[1024,1024]{1,0:T(8,128)} %shard_map.118) | data formatting | bytes 8388608

commit v3 on v2

--- a/solution.py
+++ b/solution.py
@@ -46,11 +46,11 @@
     out,
     *scratch,
 ):
-    chunks = len(scratch) - 29
-    bufs = scratch[:chunks]
+    chunks = (len(scratch) - 29) // 2
+    bufs, lasts = scratch[:chunks], scratch[chunks:2 * chunks]
     (basis, transfer, cluster, cone, pone, none, ctwo, ntwo, nlist, small_sem,
      near_f, near_h, near_l, total, part, half, share, coef, own_two, two, packed, down, dn, lift,
-     send, recv, halo_send, halo_recv, near_sem) = scratch[chunks:]
+     send, recv, halo_send, halo_recv, near_sem) = scratch[2 * chunks:]
     leaves, rank, size = basis.shape
     wide = bufs[0].shape[2]
     per_chunk = wide // LANES
@@ -92,7 +92,7 @@
     own_copies = [
         pltpu.make_async_copy(
             probes.at[:, :, pl.ds(k * wide, wide)],
-            bufs[k].at[pl.ds(leaves, leaves)],
+            bufs[k].at[pl.ds(1 + core, leaves)],
             near_sem.at[k],
         )
         for k in range(chunks)
@@ -126,17 +126,21 @@
         expected = expected + jnp.where(there, 1, 0)
     pl.semaphore_wait(barrier, expected)
 
-    def halo(k, far, l=0):
-        if far:
-            src = probes.at[pl.ds(l, 1), :, pl.ds(k * wide, wide)]
-            dst = bufs[k].at[pl.ds((1 - core) * 2 * leaves + l, 1)]
-            return remote(src, dst, halo_send.at[l, k], halo_recv.at[l, k], beside)
-        src = probes.at[:, :, pl.ds(k * wide, wide)]
-        dst = bufs[k].at[pl.ds(core * 2 * leaves, leaves)]
-        return remote(src, dst, halo_send.at[leaves, k], halo_recv.at[leaves, k], mate)
+    def halo(k, which):
+        cols = pl.ds(k * wide, wide)
+        if which == 0:
+            dst = bufs[k].at[pl.ds((1 - core) * 4, 1)]
+            src, device = probes.at[pl.ds(core, 1), :, cols], beside
+        elif which == 1:
+            dst = lasts[k]
+            src, device = probes.at[pl.ds(1 - core, 1), :, cols], beside
+        else:
+            dst = bufs[k].at[pl.ds(core * 3, leaves)]
+            src, device = probes.at[:, :, cols], mate
+        return remote(src, dst, halo_send.at[which, k], halo_recv.at[which, k], device)
 
     def piece(p):
-        pl.when(has_beside)(halo(p // leaves, True, p % leaves).start)
+        pl.when(has_beside)(halo(p // 2, p % 2).start)
 
     piece(0)
     piece(1)
@@ -151,7 +155,7 @@
     for k in range(chunks):
         own_copies[k].wait()
         value = sum(
-            dot_split(lifts[l], split(bufs[k][leaves + l]))
+            dot_split(lifts[l], split(bufs[k][1 + core + l]))
             for l in range(leaves)
         )
         for g in range(per_chunk):
@@ -196,7 +200,7 @@
         copy.start()
     coef[GROUP + c4] = share[c4]
     piece(2)
-    halo(0, False).start()
+    halo(0, 2).start()
     pack_x.wait_recv()
     pack_y.start()
 
@@ -224,14 +228,14 @@
         pl.when(reaches(o))(copy.start)
     piece(3)
     piece(4)
-    halo(1, False).start()
+    halo(1, 2).start()
     pack_y.wait_recv()
     pack_c.start()
 
     def own_near(l, _):
         at = pl.ds(pl.multiple_of(l * size, size), size)
         for k in range(chunks):
-            x = bufs[k][leaves + l]
+            x = bufs[k][1 + core + l]
             total[at, k * wide:(k + 1) * wide] = dot_split((near_h[l, 0], near_l[l, 0]), split(x))
         return _
 
@@ -282,16 +286,17 @@
     for copy in back:
         copy.start()
     piece(5)
-    halo(2, False).start()
+    halo(2, 2).start()
     dn[mine_at] = down[c4]
     for copy in back:
         copy.wait_recv()
     join = go(12, dn.at[pl.ds(quad, 4)], dn.at[pl.ds(quad, 4)], mate)
     join.start()
-    for p in range(6, chunks * leaves):
-        piece(p)
+    piece(6)
     for k in range(3, chunks):
-        halo(k, False).start()
+        halo(k, 2).start()
+    pl.when(has_beside)(halo(2, 1).wait_send)
+    piece(7)
     join.wait_recv()
 
     def far_rows(l, _):
@@ -306,23 +311,25 @@
 
     lax.fori_loop(0, leaves, far_rows, 0)
 
+    def other_near(k, l, reach):
+        at = pl.ds(pl.multiple_of(l * size, size), size)
+        value = total[at, k * wide:(k + 1) * wide]
+        for m in range(1, near.shape[1]):
+            index = nlist[l, m] - (me - 1) * leaves
+            held = jnp.maximum(0, jnp.minimum(index - 1 + core, 4))
+            x = bufs[k][held]
+            if reach:
+                x = jnp.where(index == 5 * core, lasts[k][0], x)
+            value += dot_split((near_h[l, m], near_l[l, m]), split(x))
+        total[at, k * wide:(k + 1) * wide] = value
+
     results = []
     for k in range(chunks):
-        halo(k, False).wait_recv()
-        for l in range(leaves):
-            pl.when(has_beside)(halo(k, True, l).wait_recv)
-
-        def other_near(l, _, k=k):
-            at = pl.ds(pl.multiple_of(l * size, size), size)
-            value = total[at, k * wide:(k + 1) * wide]
-            for m in range(1, near.shape[1]):
-                index = nlist[l, m] - (me - 1) * leaves
-                index = jnp.maximum(0, jnp.minimum(index, 3 * leaves - 1))
-                value += dot_split((near_h[l, m], near_l[l, m]), split(bufs[k][index]))
-            total[at, k * wide:(k + 1) * wide] = value
-            return _
-
-        lax.fori_loop(0, leaves, other_near, 0)
+        halo(k, 2).wait_recv()
+        pl.when(has_beside)(halo(k, 0).wait_recv)
+        other_near(k, 1 - core, False)
+        pl.when(has_beside)(halo(k, 1).wait_recv)
+        other_near(k, core, True)
         copy = pltpu.make_async_copy(
             total.at[:, pl.ds(k * wide, wide)],
             out.at[:, pl.ds(k * wide, wide)],
@@ -338,9 +345,10 @@
     for o, copy in two_copies:
         pl.when(reaches(o))(copy.wait_send)
     for k in range(chunks):
-        halo(k, False).wait_send()
-        for l in range(leaves):
-            pl.when(has_beside)(halo(k, True, l).wait_send)
+        halo(k, 2).wait_send()
+        pl.when(has_beside)(halo(k, 0).wait_send)
+        if k != 2:
+            pl.when(has_beside)(halo(k, 1).wait_send)
     for copy in results:
         copy.wait()
 
@@ -362,12 +370,13 @@
     small = lambda n: pltpu.VMEM((n, rank, LANES), f32)
     dma = pltpu.SemaphoreType.DMA
     flops = 2 * (near.size + 2 * basis.size) * width
-    return pl.pallas_call(
+    result = pl.pallas_call(
         functools.partial(kernel, devices, offsets),
         out_shape=jax.ShapeDtypeStruct((rows, width), f32),
         in_specs=[anywhere] * 8 + [smem] + [anywhere] * (len(args) - 9),
         out_specs=anywhere,
-        scratch_shapes=[pltpu.VMEM((3 * leaves, size, wide), f32)] * chunks
+        scratch_shapes=[pltpu.VMEM((5, size, wide), f32)] * chunks
+        + [pltpu.VMEM((1, size, wide), f32)] * chunks
         + [
             pltpu.VMEM((leaves, rank, size), f32),
             pltpu.VMEM(args[2].shape, f32),
@@ -395,8 +404,8 @@
             pltpu.VMEM((leaves, size, rank), f32),
             dma((13 + len(offsets),)),
             dma((13 + len(offsets),)),
-            dma((leaves + 1, chunks)),
-            dma((leaves + 1, chunks)),
+            dma((3, chunks)),
+            dma((3, chunks)),
             dma((chunks + 1,)),
         ],
         compiler_params=pltpu.CompilerParams(
@@ -406,6 +415,26 @@
             flops=3 * flops, bytes_accessed=4 * (near.size + 4 * probes.size), transcendentals=0
         ),
     )(probes.reshape(leaves, size, width), jnp.swapaxes(basis, 1, 2), *args[2:])
+    return pl.pallas_call(
+        hand_over,
+        out_shape=jax.ShapeDtypeStruct((rows, width), f32),
+        in_specs=[anywhere],
+        out_specs=anywhere,
+        scratch_shapes=[dma((8,))],
+    )(result)
+
+
+def hand_over(src, dst, sem):
+    parts = sem.shape[0]
+    rows = src.shape[0] // parts
+    copies = [
+        pltpu.make_async_copy(src.at[pl.ds(i * rows, rows)], dst.at[pl.ds(i * rows, rows)], sem.at[i])
+        for i in range(parts)
+    ]
+    for copy in copies:
+        copy.start()
+    for copy in copies:
+        copy.wait()
 
 
 def solution(mesh):

time: 111 us -> 236 us (2.13)
  Pallas kernels: 105 us -> 235 us
  local copies, waits for them, and re-layouts: 4.79 us -> 0 us
    pallas_call x0 -> x1, Pallas kernels: none -> 128 us  [body(): pl.pallas_call(hand_over, out_shape=jax.ShapeDtypeStruct((rows, width), f...]
    unnamed x1 -> x0, local copies, waits for them, and re-layouts: 4.79 us -> none
where the time goes in v3:
time: 236 us; the launch traced here: 235 us
  Pallas kernels  235 us (100%)
    pallas_call x1, Pallas kernels, body(): pl.pallas_call(hand_over, out_shape=jax.ShapeDtypeStruct((rows, width), f...  128 us
    pallas_call x1, Pallas kernels, body(): pl.pallas_call(functools.partial(kernel, devices, offsets), out_shape=jax...  107 us

profile of v3, /device:TPU:1, one launch (start us, length us, event | category | flops | bytes accessed | tf_op | source)
XLA Modules:
  0.0 235.5 jit_solution(2637952095389696817)
XLA Ops:
  0.7 106.6 %shard_map.118.src = f32[1024,1024]{1,0:T(8,128)} custom-call(f32[2,512,1024]{2,1,0:T(8,128)} %bitcast.2, f32[2,64,512]{2,1,0:T(8,128)} %bitcast.3, f32[2,64,64]{2,1,0:T(8,128)} %transfer_hbm.1, f32[16,64,64]{2,1,0:T(8,128)} %cluster_hbm.1, f32[4,64,64]{2,1,0:T(8,128)} %cone_hbm.1, s32[4]{0:T(128)} %pone_hbm.1, s32[16]{0:T(128)} %none_hbm.1, ...), custom_call_target="tpu_custom_call" | custom-call | flops 10468982784 | bytes 23068672 | tf_op jit(solution)/shard_map/pallas_call | solution.py:373
  107.2 128.2 %shard_map.119 = f32[1024,1024]{1,0:T(8,128)} custom-call(f32[1024,1024]{1,0:T(8,128)} %shard_map.118.src), custom_call_target="tpu_custom_call" | custom-call | tf_op jit(solution)/shard_map/pallas_call | solution.py:418

commit v4 on v2

--- a/solution.py
+++ b/solution.py
@@ -136,7 +136,8 @@
         return remote(src, dst, halo_send.at[leaves, k], halo_recv.at[leaves, k], mate)
 
     def piece(p):
-        pl.when(has_beside)(halo(p // leaves, True, p % leaves).start)
+        copy = halo(p // leaves, True, p % leaves)
+        pl.when(has_beside)(copy.start)
 
     piece(0)
     piece(1)
@@ -224,6 +225,7 @@
         pl.when(reaches(o))(copy.start)
     piece(3)
     piece(4)
+    piece(5)
     halo(1, False).start()
     pack_y.wait_recv()
     pack_c.start()
@@ -281,14 +283,14 @@
     ]
     for copy in back:
         copy.start()
-    piece(5)
+    piece(6)
     halo(2, False).start()
     dn[mine_at] = down[c4]
     for copy in back:
         copy.wait_recv()
     join = go(12, dn.at[pl.ds(quad, 4)], dn.at[pl.ds(quad, 4)], mate)
     join.start()
-    for p in range(6, chunks * leaves):
+    for p in range(7, chunks * leaves):
         piece(p)
     for k in range(3, chunks):
         halo(k, False).start()
@@ -362,7 +364,7 @@
     small = lambda n: pltpu.VMEM((n, rank, LANES), f32)
     dma = pltpu.SemaphoreType.DMA
     flops = 2 * (near.size + 2 * basis.size) * width
-    return pl.pallas_call(
+    result = pl.pallas_call(
         functools.partial(kernel, devices, offsets),
         out_shape=jax.ShapeDtypeStruct((rows, width), f32),
         in_specs=[anywhere] * 8 + [smem] + [anywhere] * (len(args) - 9),
@@ -406,6 +408,31 @@
             flops=3 * flops, bytes_accessed=4 * (near.size + 4 * probes.size), transcendentals=0
         ),
     )(probes.reshape(leaves, size, width), jnp.swapaxes(basis, 1, 2), *args[2:])
+    return pl.pallas_call(
+        hand_over,
+        out_shape=jax.ShapeDtypeStruct((rows, width), f32),
+        in_specs=[anywhere],
+        out_specs=anywhere,
+        scratch_shapes=[pltpu.VMEM((rows, width), f32), dma((8,)), dma((8,))],
+        compiler_params=pltpu.CompilerParams(vmem_limit_bytes=32 * 1024 * 1024),
+    )(result)
+
+
+def hand_over(src, dst, held, arrived, left):
+    parts = arrived.shape[0]
+    rows = src.shape[0] // parts
+    at = [pl.ds(i * rows, rows) for i in range(parts)]
+    into = [
+        pltpu.make_async_copy(src.at[at[i]], held.at[at[i]], arrived.at[i]) for i in range(parts)
+    ]
+    away = [pltpu.make_async_copy(held.at[at[i]], dst.at[at[i]], left.at[i]) for i in range(parts)]
+    for copy in into:
+        copy.start()
+    for i in range(parts):
+        into[i].wait()
+        away[i].start()
+    for copy in away:
+        copy.wait()
 
 
 def solution(mesh):

time: 111 us -> 111 us (level)
  Pallas kernels: 105 us -> 108 us
  local copies, waits for them, and re-layouts: 4.79 us -> 2.18 us
    unnamed x1 -> x2, local copies, waits for them, and re-layouts: 4.79 us -> 2.18 us
    pallas_call x0 -> x1, Pallas kernels: none -> 2.42 us  [body(): pl.pallas_call(hand_over, out_shape=jax.ShapeDtypeStruct((rows, width), f...]
where the time goes in v4:
time: 111 us; the launch traced here: 110 us
  Pallas kernels  108 us (97%)
  local copies, waits for them, and re-layouts  2.18 us (2%)
    pallas_call x1, Pallas kernels, body(): pl.pallas_call(functools.partial(kernel, devices, offsets), out_shape=jax...  105 us
    pallas_call x1, Pallas kernels, body(): pl.pallas_call(hand_over, out_shape=jax.ShapeDtypeStruct((rows, width), f...  2.42 us

profile of v4, /device:TPU:1, one launch (start us, length us, event | category | flops | bytes accessed | tf_op | source)
XLA Modules:
  0.0 110.4 jit_solution(9821478500061710065)
XLA Ops:
  0.7 105.2 %shard_map.118.src = f32[1024,1024]{1,0:T(8,128)} custom-call(f32[2,512,1024]{2,1,0:T(8,128)} %bitcast.2, f32[2,64,512]{2,1,0:T(8,128)} %bitcast.3, f32[2,64,64]{2,1,0:T(8,128)} %transfer_hbm.1, f32[16,64,64]{2,1,0:T(8,128)} %cluster_hbm.1, f32[4,64,64]{2,1,0:T(8,128)} %cone_hbm.1, s32[4]{0:T(128)} %pone_hbm.1, s32[16]{0:T(128)} %none_hbm.1, ...), custom_call_target="tpu_custom_call" | custom-call | flops 10468982784 | bytes 23068672 | tf_op jit(solution)/shard_map/pallas_call | solution.py:367
  105.8 0.0 copy-start
  105.8 2.2 %copy-done = f32[1024,1024]{1,0:T(8,128)S(1)} copy-done((f32[1024,1024]{1,0:T(8,128)S(1)}, f32[1024,1024]{1,0:T(8,128)}, u32[]{:S(2)}) %copy-start) | copy-done | bytes 4194328
  108.0 2.4 %shard_map.119 = f32[1024,1024]{1,0:T(8,128)} custom-call(f32[1024,1024]{1,0:T(8,128)S(1)} %copy-done), custom_call_target="tpu_custom_call" | custom-call | tf_op jit(solution)/shard_map/pallas_call | solution.py:411
Async XLA Ops:
  105.8 2.2 %copy-start = (f32[1024,1024]{1,0:T(8,128)S(1)}, f32[1024,1024]{1,0:T(8,128)}, u32[]{:S(2)}) copy-start(f32[1024,1024]{1,0:T(8,128)} %shard_map.118.src) | copy-start | bytes 12582916

commit v5 on v4

--- a/solution.py
+++ b/solution.py
@@ -168,7 +168,9 @@
         packed[slot, pl.ds(s * rank, rank), :] = jnp.concatenate(
             [cone[2 * s], cone[2 * s + 1]], axis=1
         )
-    packed[slot, pl.ds(slots // 2 * rank, rank), :] = jnp.concatenate([ctwo[0], ctwo[0]], axis=1)
+    packed[slot, pl.ds(slots // 2 * rank, rank // 2), :] = jnp.concatenate(
+        [ctwo[0, : rank // 2], ctwo[0, rank // 2 :]], axis=1
+    )
     mine = q * GROUP + c4
     ids = [
         jnp.where(core * slots + k < none[mine], pone[k], -1) for k in range(slots)
@@ -178,7 +180,7 @@
     table = jnp.full((8, LANES), -1, jnp.int32)
     for k, value in enumerate(ids):
         table = jnp.where(row == k, value, table)
-    id_row = slots // 2 * rank + rank
+    id_row = slots // 2 * rank + rank // 2
     packed[slot, pl.ds(id_row, 8), :] = table.astype(jnp.float32)
     bit_x, bit_y = lax.rem(c4, 2), lax.div(c4, 2)
     pack_x = go(6, packed.at[pl.ds(slot, 1)], packed.at[pl.ds(slot, 1)], chip(xor(c4, 1)))
@@ -225,7 +227,6 @@
         pl.when(reaches(o))(copy.start)
     piece(3)
     piece(4)
-    piece(5)
     halo(1, False).start()
     pack_y.wait_recv()
     pack_c.start()
@@ -257,9 +258,9 @@
     far_two = zero
     for at in range(plane_size):
         options = [(q + o, two[i]) for i, o in enumerate(offsets)]
-        far_two += dot(
-            packed[at, pl.ds(slots // 2 * rank, rank), :][:, :rank], chosen(at, slots, options)
-        )
+        folded = packed[at, pl.ds(slots // 2 * rank, rank // 2), :]
+        block = jnp.concatenate([folded[:, :rank], folded[:, rank:]], axis=0)
+        far_two += dot(block, chosen(at, slots, options))
 
     far_two_split = split(far_two)
 
@@ -283,14 +284,14 @@
     ]
     for copy in back:
         copy.start()
-    piece(6)
+    piece(5)
     halo(2, False).start()
     dn[mine_at] = down[c4]
     for copy in back:
         copy.wait_recv()
     join = go(12, dn.at[pl.ds(quad, 4)], dn.at[pl.ds(quad, 4)], mate)
     join.start()
-    for p in range(7, chunks * leaves):
+    for p in range(6, chunks * leaves):
         piece(p)
     for k in range(3, chunks):
         halo(k, False).start()
@@ -391,7 +392,7 @@
             small(3 * GROUP),
             pltpu.VMEM((rank, LANES), f32),
             small(max(1, len(offsets))),
-            pltpu.VMEM((2 * GROUP, (slots // 2 + 1) * rank + 8, LANES), f32),
+            pltpu.VMEM((2 * GROUP, slots // 2 * rank + rank // 2 + 8, LANES), f32),
             small(GROUP),
             small(groups),
             pltpu.VMEM((leaves, size, rank), f32),
@@ -413,8 +414,8 @@
         out_shape=jax.ShapeDtypeStruct((rows, width), f32),
         in_specs=[anywhere],
         out_specs=anywhere,
-        scratch_shapes=[pltpu.VMEM((rows, width), f32), dma((8,)), dma((8,))],
-        compiler_params=pltpu.CompilerParams(vmem_limit_bytes=32 * 1024 * 1024),
+        scratch_shapes=[pltpu.VMEM((rows, width), f32), dma((16,)), dma((16,))],
+        compiler_params=pltpu.CompilerParams(vmem_limit_bytes=64 * 1024 * 1024 - 64 * 1024),
     )(result)
 
 

time: 111 us -> 109 us (0.982)
  local copies, waits for them, and re-layouts: 2.18 us -> 0 us
    unnamed x2 -> x0, local copies, waits for them, and re-layouts: 2.18 us -> none
    pallas_call x1, Pallas kernels: 2.42 us -> 3.85 us  [body(): pl.pallas_call(hand_over, out_shape=jax.ShapeDtypeStruct((rows, width), f...]
where the time goes in v5:
time: 109 us
  Pallas kernels  109 us (100%)
    pallas_call x1, Pallas kernels, body(): pl.pallas_call(functools.partial(kernel, devices, offsets), out_shape=jax...  105 us
    pallas_call x1, Pallas kernels, body(): pl.pallas_call(hand_over, out_shape=jax.ShapeDtypeStruct((rows, width), f...  3.85 us

profile of v5, /device:TPU:1, one launch (start us, length us, event | category | flops | bytes accessed | tf_op | source)
XLA Modules:
  0.0 109.3 jit_solution(3722822576513234194)
XLA Ops:
  0.7 104.8 %shard_map.118.src = f32[1024,1024]{1,0:T(8,128)} custom-call(f32[2,512,1024]{2,1,0:T(8,128)} %bitcast.2, f32[2,64,512]{2,1,0:T(8,128)} %bitcast.3, f32[2,64,64]{2,1,0:T(8,128)} %transfer_hbm.1, f32[16,64,64]{2,1,0:T(8,128)} %cluster_hbm.1, f32[4,64,64]{2,1,0:T(8,128)} %cone_hbm.1, s32[4]{0:T(128)} %pone_hbm.1, s32[16]{0:T(128)} %none_hbm.1, ...), custom_call_target="tpu_custom_call" | custom-call | flops 10468982784 | bytes 23068672 | tf_op jit(solution)/shard_map/pallas_call | solution.py:368
  105.5 3.9 %shard_map.119 = f32[1024,1024]{1,0:T(8,128)} custom-call(f32[1024,1024]{1,0:T(8,128)} %shard_map.118.src), custom_call_target="tpu_custom_call" | custom-call | tf_op jit(solution)/shard_map/pallas_call | solution.py:412

commit v6 on v5

--- a/solution.py
+++ b/solution.py
@@ -325,14 +325,18 @@
             total[at, k * wide:(k + 1) * wide] = value
             return _
 
-        lax.fori_loop(0, leaves, other_near, 0)
-        copy = pltpu.make_async_copy(
-            total.at[:, pl.ds(k * wide, wide)],
-            out.at[:, pl.ds(k * wide, wide)],
-            near_sem.at[k],
-        )
-        copy.start()
-        results.append(copy)
+        groups = leaves if k == chunks - 1 else 1
+        tall = leaves // groups
+        for l in range(groups):
+            lax.fori_loop(l * tall, (l + 1) * tall, other_near, 0)
+            at = pl.ds(l * tall * size, tall * size)
+            copy = pltpu.make_async_copy(
+                total.at[at, pl.ds(k * wide, wide)],
+                out.at[at, pl.ds(k * wide, wide)],
+                near_sem.at[k + l],
+            )
+            copy.start()
+            results.append(copy)
 
     for copy in [halve, pack_x, pack_y, pack_c, join] + spread + back:
         copy.wait_send()

time: 109 us -> 109 us (level)
  no operation moved by 1% of the time
where the time goes in v6:
time: 109 us
  Pallas kernels  109 us (100%)
    pallas_call x1, Pallas kernels, body(): pl.pallas_call(functools.partial(kernel, devices, offsets), out_shape=jax...  105 us
    pallas_call x1, Pallas kernels, body(): pl.pallas_call(hand_over, out_shape=jax.ShapeDtypeStruct((rows, width), f...  3.85 us

profile of v6, /device:TPU:1, one launch (start us, length us, event | category | flops | bytes accessed | tf_op | source)
XLA Modules:
  0.0 109.2 jit_solution(1669788384284381873)
XLA Ops:
  0.7 104.7 %shard_map.118.src = f32[1024,1024]{1,0:T(8,128)} custom-call(f32[2,512,1024]{2,1,0:T(8,128)} %bitcast.2, f32[2,64,512]{2,1,0:T(8,128)} %bitcast.3, f32[2,64,64]{2,1,0:T(8,128)} %transfer_hbm.1, f32[16,64,64]{2,1,0:T(8,128)} %cluster_hbm.1, f32[4,64,64]{2,1,0:T(8,128)} %cone_hbm.1, s32[4]{0:T(128)} %pone_hbm.1, s32[16]{0:T(128)} %none_hbm.1, ...), custom_call_target="tpu_custom_call" | custom-call | flops 10468982784 | bytes 23068672 | tf_op jit(solution)/shard_map/pallas_call | solution.py:372
  105.3 3.9 %shard_map.119 = f32[1024,1024]{1,0:T(8,128)} custom-call(f32[1024,1024]{1,0:T(8,128)} %shard_map.118.src), custom_call_target="tpu_custom_call" | custom-call | tf_op jit(solution)/shard_map/pallas_call | solution.py:416
